TPU v7x, 32 devices: a whole 2x2x4 slice. The times are simulated.
32 devices in a mesh: group: 2 (over x), ep: 16 (over z, y, core).
Axes of the slice: x: 2, y: 2, z: 4, core: 2. Of those that a mesh axis runs over, the one named last changes fastest.
Arguments:
- tokens: bfloat16 [2048, 3584], P(('group', 'ep')), parts along dimension 0, may hold values from -6 to 6
- expert_ids: int32 [2048, 4], P(('group', 'ep')), parts along dimension 0, may hold values from 0 to 7, all different within a row; in each aligned block of 64 rows (0 to 63, 64 to 127, ...) at most 36 rows name the same one
- gate_weights: float32 [2048, 4], P(('group', 'ep')), parts along dimension 0, may hold values from 0.1 to 0.5
- w_gate: bfloat16 [3584, 8192], P(None, 'ep'), may hold values from -0.09375 to 0.09375
- w_up: bfloat16 [3584, 8192], P(None, 'ep'), may hold values from -0.09375 to 0.09375
- w_down: bfloat16 [8192, 3584], P('ep'), may hold values from -0.1875 to 0.1875
- prefill_latent: bfloat16 [2048, 576], P(('group', 'ep')), parts along dimension 0, may hold values from -6 to 6
- page_target: int32 [128], P(('group', 'ep')), parts along dimension 0, may hold values from 0 to 15, as said below
- queries: bfloat16 [32, 64, 576], P(('group', 'ep')), parts along dimension 0, may hold values from -400 to 400
- cache_latent: bfloat16 [32, 256, 576], P(('group', 'ep')), parts along dimension 0, may hold values from -7 to 7
- cache_len: int32 [32], P(('group', 'ep')), parts along dimension 0, may hold values from 1 to 256, 2048 in all
Outputs:
- moe_out: bfloat16 [2048, 3584], P(('group', 'ep')), parts along dimension 0
- attn_out: bfloat16 [32, 64, 512], P(('group', 'ep')), parts along dimension 0
There are 2 independent parts, one for each index of `group`. A program takes and returns all parts, laid end to end along the dimension named above; an argument that names none is the same for every part. Nothing has to cross between parts.
Inputs may be any that keep to these rules, and one draw needn't show every extreme that they name: `expert_ids`: each row names 4 different experts; among the rows of one device no expert is named by more than 36 rows. `page_target`: request r belongs to the device with index r // 1 along ep. The pages of one device name requests of pairwise different devices; some request is named by one page of every device. `cache_len`: some request holds exactly 256 positions.
All inputs are finite; a program needn't handle non-finite values. No bound on the sum of `cache_len` on one device may be relied on, other than what follows from the above.
Results may differ from a plain program's by a relative error of at most 0.008.
Values may be sent and summed in bfloat16 or wider, within the bound.
A program may use at most 128 MiB of HBM per device.

v0:
```python
import jax
import jax.numpy as jnp
from jax import lax
from jax.sharding import PartitionSpec as P

SPLIT = 2
LAT = 512
PAGE = 16


score_scale = 192.0 ** (-0.5)
mask_low = -1e30


def expert_rows(rows, w_gate, w_up, w_down):
    gate = jnp.dot(rows, w_gate, preferred_element_type=jnp.float32)
    upward = jnp.dot(rows, w_up, preferred_element_type=jnp.float32)
    hidden = (jax.nn.silu(gate) * upward).astype(jnp.bfloat16)
    return jnp.dot(hidden, w_down, preferred_element_type=jnp.float32).astype(jnp.bfloat16)


def experts_part(tokens, expert_ids, gate_weights, w_gate, w_up, w_down):
    owners = lax.axis_size("ep")
    experts = owners // SPLIT
    tok_count, width = tokens.shape
    topk = expert_ids.shape[1]
    capacity = max(2, (9 * tok_count * topk + 8 * experts - 1) // (8 * experts))
    flat = expert_ids.reshape(-1)
    onehot = (flat[:, None] == jnp.arange(experts, dtype=jnp.int32)[None, :]).astype(jnp.int32)
    before = jnp.cumsum(onehot, axis=0) - onehot
    slot = jnp.sum(before * onehot, axis=1)
    target = flat * capacity + slot
    repeated = jnp.repeat(tokens, topk, axis=0)
    per_expert = jnp.zeros((experts * capacity, width), jnp.bfloat16).at[target].set(repeated)
    outgoing = jnp.broadcast_to(
        per_expert.reshape(experts, 1, capacity, width), (experts, SPLIT, capacity, width)
    )
    outgoing = outgoing.reshape(owners, capacity, width)
    arrived = lax.all_to_all(outgoing, "ep", split_axis=0, concat_axis=0, tiled=True)
    count = arrived.shape[1]
    done = expert_rows(arrived.reshape(-1, width), w_gate, w_up, w_down)
    back = lax.all_to_all(
        done.reshape(owners, count, width), "ep", split_axis=0, concat_axis=0, tiled=True
    )
    grouped = back.reshape(experts, SPLIT, capacity, width)
    picked = grouped[flat, :, slot]
    summed = jnp.sum(picked.astype(jnp.float32), axis=1).reshape(tok_count, topk, width)
    mixed = jnp.sum(gate_weights[:, :, None] * summed, axis=1)
    return mixed.astype(jnp.bfloat16)


def decode_part(prefill_latent, page_target, queries, cache_latent, cache_len):
    dec_count = queries.shape[0]
    positions = cache_latent.shape[1]
    mine = lax.axis_index("ep") * dec_count + jnp.arange(dec_count, dtype=jnp.int32)
    scores = (
        jnp.einsum("rhk,rck->rhc", queries, cache_latent, preferred_element_type=jnp.float32)
        * score_scale
    )
    valid = (jnp.arange(positions, dtype=jnp.int32)[None, :] < cache_len[:, None])[:, None, :]
    peak = jnp.max(jnp.where(valid, scores, mask_low), axis=2)
    weight = jnp.where(valid, jnp.exp(scores - peak[:, :, None]), 0.0)
    total = jnp.sum(weight, axis=2)
    summed = jnp.einsum(
        "rhc,rcv->rhv",
        weight.astype(jnp.bfloat16),
        cache_latent[:, :, :LAT],
        preferred_element_type=jnp.float32,
    )
    old_summed = summed
    latent_rows = lax.all_gather(prefill_latent, "ep", axis=0, tiled=True)
    page_owner = lax.all_gather(page_target, "ep", axis=0, tiled=True)
    row_target = jnp.repeat(page_owner, PAGE)
    match = (row_target[None, :] == mine[:, None])[:, None, :]
    piece_scores = (
        jnp.einsum("rhk,tk->rht", queries, latent_rows, preferred_element_type=jnp.float32)
        * score_scale
    )
    piece_peak = jnp.max(jnp.where(match, piece_scores, mask_low), axis=2)
    new_peak = jnp.maximum(peak, piece_peak)
    piece_weight = jnp.where(match, jnp.exp(piece_scores - new_peak[:, :, None]), 0.0)
    shrink = jnp.exp(peak - new_peak)
    new_total = total * shrink + jnp.sum(piece_weight, axis=2)
    added = jnp.einsum(
        "rht,tv->rhv",
        piece_weight.astype(jnp.bfloat16),
        latent_rows[:, :LAT],
        preferred_element_type=jnp.float32,
    )
    summed = old_summed * shrink[:, :, None] + added
    return (summed / new_total[:, :, None]).astype(jnp.bfloat16)


def local(
    tokens,
    expert_ids,
    gate_weights,
    w_gate,
    w_up,
    w_down,
    prefill_latent,
    page_target,
    queries,
    cache_latent,
    cache_len,
):
    moe_out = experts_part(tokens, expert_ids, gate_weights, w_gate, w_up, w_down)
    attn_out = decode_part(prefill_latent, page_target, queries, cache_latent, cache_len)
    return (moe_out, attn_out)


def solution(mesh):
    placed = (
        P(("group", "ep"), None),
        P(("group", "ep"), None),
        P(("group", "ep"), None),
        P(None, "ep"),
        P(None, "ep"),
        P("ep", None),
        P(("group", "ep"), None),
        P(("group", "ep")),
        P(("group", "ep"), None, None),
        P(("group", "ep"), None, None),
        P(("group", "ep")),
    )
    return jax.shard_map(
        local,
        mesh=mesh,
        in_specs=placed,
        out_specs=(P(("group", "ep"), None), P(("group", "ep"), None, None)),
        check_vma=False,
    )
```

profile of v0, /device:TPU:0, one launch (start us, length us, event | category | flops | bytes accessed | tf_op | source)
XLA Modules:
  0.0 336.5 jit_solution(12709426211976584465)
XLA Ops:
  7.2 0.8 copy.30
  8.3 0.6 reduce-window.6
  9.2 1.5 broadcast_in_dim.66
  10.7 1.5 reshape.246
  12.2 5.6 %scatter_custom_fusion = bf16[288,3584]{1,0:T(8,128)(2,1)} fusion(s32[256]{0:T(256)S(1)} %bitcast.44, bf16[256,3584]{1,0:T(8,128)(2,1)} %reshape.246, bf16[]{:T(256)} %constant.11.clone.1), kind=kCustom, calls=%fused_computation.15 | custom fusion | bytes 2064896 | tf_op jit(solution)/shard_map/scatter | solution.py:34
  17.8 2.5 broadcast_in_dim.67
  20.3 0.4 broadcast_in_dim.68
  20.7 108.5 %all_to_all.10 = bf16[16,36,3584]{2,1,0:T(8,128)(2,1)} all-to-all(bf16[16,36,3584]{2,1,0:T(8,128)(2,1)S(1)} %bitcast.41), channel_id=1, replica_groups=mesh['group'=2,'ep'=16] {'ep'}, dimensions={0} | all-to-all | bytes 8257536 | tf_op jit(solution)/shard_map/all_to_all | solution.py:39
  129.2 7.0 %reshape.229 = bf16[576,3584]{1,0:T(8,128)(2,1)} reshape(bf16[16,36,3584]{2,1,0:T(8,128)(2,1)} %all_to_all.10) | data formatting | bytes 8257536 | tf_op jit(solution)/shard_map/reshape | solution.py:41
  136.2 5.6 %fusion.36 = f32[576,512]{1,0:T(8,128)S(1)} fusion(bf16[576,3584]{1,0:T(8,128)(2,1)} %reshape.229, bf16[3584,512]{1,0:T(8,128)(2,1)} %param.14), kind=kOutput, calls=%fused_computation.59 | convolution fusion | flops 2113929216 | bytes 8978432 | tf_op jit(solution)/shard_map/dot_general | solution.py:16
  141.8 10.8 %convolution_convert_fusion = bf16[576,3584]{1,0:T(8,128)(2,1)} fusion(bf16[512,3584]{1,0:T(8,128)(2,1)} %param.16, bf16[576,3584]{1,0:T(8,128)(2,1)} %reshape.229, bf16[3584,512]{1,0:T(8,128)(2,1)} %param.15, f32[576,512]{1,0:T(8,128)S(1)} %fusion.36), kind=kOutput, calls=%fused_computation.3 | convolution fusion | flops 4231692288 | bytes 16777216 | tf_op jit(solution)/shard_map/dot_general | solution.py:19
  152.6 6.9 %reshape.230 = bf16[16,36,3584]{2,1,0:T(8,128)(2,1)} reshape(bf16[576,3584]{1,0:T(8,128)(2,1)} %convolution_convert_fusion) | data formatting | bytes 8257536 | tf_op jit(solution)/shard_map/reshape | solution.py:43
  159.5 5.0 %all-to-all-start.1 = ((bf16[16,36,3584]{2,1,0:T(8,128)(2,1)}), bf16[16,36,3584]{2,1,0:T(8,128)(2,1)}, u32[]{:S(2)}, u32[]{:S(2)}) async-start(bf16[16,36,3584]{2,1,0:T(8,128)(2,1)} %reshape.230), calls=%async_computation.1 | async-start | bytes 9175040 | tf_op jit(solution)/shard_map/all_to_all | solution.py:42
  164.6 0.7 all-gather.2.cloned.1.call-update
  165.4 0.6 dynamic-slice
  166.9 108.2 %all-reduce = s32[64]{0:T(128)S(1)} all-reduce(s32[64]{0:T(128)S(1)} %dynamic-update-slice), channel_id=1, replica_groups=mesh['group'=2,'ep'=16] {'ep'}, use_global_device_ids=true, to_apply=%add | all-reduce | flops 64 | bytes 512
  275.9 0.3 select_reduce_fusion.1
  276.4 1.9 select_reduce_fusion
  278.8 2.2 fusion.3
  281.0 7.4 %copy.34 = bf16[8,2,36,3584]{3,1,2,0:T(2,128)(2,1)} copy(bf16[8,2,36,3584]{3,2,1,0:T(8,128)(2,1)} %bitcast.5) | data formatting | bytes 8257536 | tf_op jit(solution)/shard_map/reshape | solution.py:45
  288.5 17.5 %gather_fusion = bf16[256,2,3584]{2,1,0:T(2,128)(2,1)} fusion(bf16[8,2,36,3584]{3,1,2,0:T(2,128)(2,1)} %copy.34, s32[256]{0:T(256)S(1)} %bitcast.42), kind=kCustom, calls=%fused_computation | custom fusion | bytes 7342080 | tf_op jit(solution)/shard_map/gather | solution.py:46
  306.0 13.1 %convert_reduce_fusion = f32[256,3584]{1,0:T(8,128)} fusion(bf16[256,2,3584]{2,1,0:T(2,128)(2,1)} %gather_fusion), kind=kLoop, calls=%fused_computation.2 | loop fusion | flops 2752512 | bytes 7340032 | tf_op jit(solution)/shard_map/reduce_sum | solution.py:47
  319.1 5.2 %reshape.232 = f32[64,4,3584]{2,1,0:T(4,128)} reshape(f32[256,3584]{1,0:T(8,128)} %convert_reduce_fusion) | data formatting | bytes 7340032 | tf_op jit(solution)/shard_map/reshape | solution.py:47
  324.3 5.3 %multiply_reduce_fusion = bf16[64,3584]{1,0:T(8,128)(2,1)} fusion(f32[64,4,3584]{2,1,0:T(4,128)} %reshape.232, f32[64,4]{1,0:T(8,128)S(1)} %copy.29), kind=kLoop, calls=%fused_computation.4 | loop fusion | flops 1605632 | bytes 4129792 | tf_op jit(solution)/shard_map/reduce_sum | solution.py:48
  (34 shorter events, 1.9 us)
Async XLA Ops:
  7.2 268.7 %copy-start = (bf16[1,64,576]{2,1,0:T(8,128)(2,1)S(1)}, bf16[1,64,576]{2,1,0:T(8,128)(2,1)}, u32[]{:S(2)}) copy-start(bf16[1,64,576]{2,1,0:T(8,128)(2,1)} %param.19) | copy-start | bytes 221188
  159.5 5.8 %copy-start.2 = (f32[64,4]{0,1:T(4,128)S(1)}, f32[64,4]{0,1:T(4,128)}, u32[]{:S(2)}) copy-start(f32[64,4]{0,1:T(4,128)} %param.13) | copy-start | bytes 3076
  159.5 5.9 %copy-start.4 = (u32[32]{0:T(128)S(1)}, u32[32]{0:T(128)}, u32[]{:S(2)}) copy-start(u32[32]{0:T(128)} %constant.50) | copy-start | bytes 388
  159.5 7.1 %copy-start.3 = (s32[4]{0:T(128)S(1)}, s32[4]{0:T(128)}, u32[]{:S(2)}) copy-start(s32[4]{0:T(128)} %param.18) | copy-start | bytes 52
  159.5 116.4 %copy-start.1 = (bf16[1,256,576]{1,2,0:T(8,128)(2,1)S(1)}, bf16[1,256,576]{1,2,0:T(8,128)(2,1)}, u32[]{:S(2)}) copy-start(bf16[1,256,576]{1,2,0:T(8,128)(2,1)} %param.20) | copy-start | bytes 884740
  159.5 121.5 %all-to-all-start.1 = ((bf16[16,36,3584]{2,1,0:T(8,128)(2,1)}), bf16[16,36,3584]{2,1,0:T(8,128)(2,1)}, u32[]{:S(2)}, u32[]{:S(2)}) async-start(bf16[16,36,3584]{2,1,0:T(8,128)(2,1)} %reshape.230), calls=%async_computation.1 | async-start | bytes 9175040 | tf_op jit(solution)/shard_map/all_to_all | solution.py:42
  164.5 111.9 %all-gather.2.cloned.1.call-start = ((), (), s32[]{:S(2)}) async-start(), calls=%async_computation.2 | async-start | bytes 1392640 | tf_op jit(solution)/shard_map/all_gather | solution.py:71
Sparse Core Ops, SparseCore 0:
  167.6 82.6 all-gather.1
where the time goes:
time: 337 us; the launch traced here: 336 us
  blocking collectives  217 us (64%)
  local copies, waits for them, and re-layouts  57.9 us (17%)
  matrix products  21 us (6%)
  other arithmetic  19.6 us (6%)
  between operations  15.5 us (5%)
  starting transfers between devices  5.04 us (1%)
    all_to_all x1, blocking collectives, experts_part(): lax.all_to_all(outgoing, 'ep', split_axis=0, concat_axis=0, tiled=True)  109 us
    unnamed x1, blocking collectives  108 us
    gather x1, local copies, waits for them, and re-layouts, experts_part(): picked = grouped[flat, :, slot]  17.5 us
    reduce_sum x1, other arithmetic, experts_part(): jnp.sum(picked.astype(jnp.float32), axis=1).reshape(tok_count, topk, width)  13.1 us
    dot_general x1, matrix products, expert_rows(): jnp.dot(hidden, w_down, preferred_element_type=jnp.float32)  10.8 us
    reshape x1, local copies, waits for them, and re-layouts, experts_part(): grouped = back.reshape(experts, SPLIT, capacity, width)  7.45 us
    reshape x1, local copies, waits for them, and re-layouts, experts_part(): done = expert_rows(arrived.reshape(-1, width), w_gate, w_up, w_down)  6.97 us
    reshape x1, local copies, waits for them, and re-layouts, experts_part(): done.reshape(owners, count, width)  6.92 us
  transfers between devices with their start and end apart: 2, of which 0 were waited for; matrix products, arithmetic and copies ran while one was open for 2% of the time, Pallas kernels for 0%

commit v1 on v0

--- a/solution.py
+++ b/solution.py
@@ -12,41 +12,27 @@
 mask_low = -1e30
 
 
-def expert_rows(rows, w_gate, w_up, w_down):
+def experts_part(tokens, expert_ids, gate_weights, w_gate, w_up, w_down):
+    owners = lax.axis_size("ep")
+    experts = owners // SPLIT
+    flat = jnp.sum(
+        jnp.where(
+            expert_ids[:, :, None] == jnp.arange(experts, dtype=jnp.int32)[None, None, :],
+            gate_weights[:, :, None],
+            0.0,
+        ),
+        axis=1,
+    )
+    rows = lax.all_gather(tokens, "ep", axis=0, tiled=True)
+    mixing = lax.all_to_all(
+        jnp.repeat(flat.T, SPLIT, axis=0), "ep", split_axis=0, concat_axis=0, tiled=True
+    ).reshape(-1)
     gate = jnp.dot(rows, w_gate, preferred_element_type=jnp.float32)
     upward = jnp.dot(rows, w_up, preferred_element_type=jnp.float32)
     hidden = (jax.nn.silu(gate) * upward).astype(jnp.bfloat16)
-    return jnp.dot(hidden, w_down, preferred_element_type=jnp.float32).astype(jnp.bfloat16)
-
-
-def experts_part(tokens, expert_ids, gate_weights, w_gate, w_up, w_down):
-    owners = lax.axis_size("ep")
-    experts = owners // SPLIT
-    tok_count, width = tokens.shape
-    topk = expert_ids.shape[1]
-    capacity = max(2, (9 * tok_count * topk + 8 * experts - 1) // (8 * experts))
-    flat = expert_ids.reshape(-1)
-    onehot = (flat[:, None] == jnp.arange(experts, dtype=jnp.int32)[None, :]).astype(jnp.int32)
-    before = jnp.cumsum(onehot, axis=0) - onehot
-    slot = jnp.sum(before * onehot, axis=1)
-    target = flat * capacity + slot
-    repeated = jnp.repeat(tokens, topk, axis=0)
-    per_expert = jnp.zeros((experts * capacity, width), jnp.bfloat16).at[target].set(repeated)
-    outgoing = jnp.broadcast_to(
-        per_expert.reshape(experts, 1, capacity, width), (experts, SPLIT, capacity, width)
-    )
-    outgoing = outgoing.reshape(owners, capacity, width)
-    arrived = lax.all_to_all(outgoing, "ep", split_axis=0, concat_axis=0, tiled=True)
-    count = arrived.shape[1]
-    done = expert_rows(arrived.reshape(-1, width), w_gate, w_up, w_down)
-    back = lax.all_to_all(
-        done.reshape(owners, count, width), "ep", split_axis=0, concat_axis=0, tiled=True
-    )
-    grouped = back.reshape(experts, SPLIT, capacity, width)
-    picked = grouped[flat, :, slot]
-    summed = jnp.sum(picked.astype(jnp.float32), axis=1).reshape(tok_count, topk, width)
-    mixed = jnp.sum(gate_weights[:, :, None] * summed, axis=1)
-    return mixed.astype(jnp.bfloat16)
+    done = jnp.dot(hidden, w_down, preferred_element_type=jnp.float32)
+    done = (done * mixing[:, None]).astype(jnp.bfloat16)
+    return lax.psum_scatter(done, "ep", scatter_dimension=0, tiled=True)
 
 
 def decode_part(prefill_latent, page_target, queries, cache_latent, cache_len):
@@ -91,19 +77,7 @@
     return (summed / new_total[:, :, None]).astype(jnp.bfloat16)
 
 
-def local(
-    tokens,
-    expert_ids,
-    gate_weights,
-    w_gate,
-    w_up,
-    w_down,
-    prefill_latent,
-    page_target,
-    queries,
-    cache_latent,
-    cache_len,
-):
+def local(tokens, expert_ids, gate_weights, w_gate, w_up, w_down, prefill_latent, page_target, queries, cache_latent, cache_len):
     moe_out = experts_part(tokens, expert_ids, gate_weights, w_gate, w_up, w_down)
     attn_out = decode_part(prefill_latent, page_target, queries, cache_latent, cache_len)
     return (moe_out, attn_out)

time: 337 us -> 223 us (0.66)
  blocking collectives: 217 us -> 9.81 us
  waiting for transfers between devices: 0.7 us -> 159 us
  local copies, waits for them, and re-layouts: 57.9 us -> 2.81 us
  other arithmetic: 19.6 us -> 1.82 us
  matrix products: 21 us -> 26.3 us
    all_to_all x1 -> x0, blocking collectives: 109 us -> none  [experts_part(): lax.all_to_all(outgoing, 'ep', split_axis=0, concat_axis=0, tiled=True)]
    unnamed x1, blocking collectives: 108 us -> 9.81 us
    reduce_scatter x0 -> x1, waiting for transfers between devices: none -> 90.7 us  [experts_part(): return lax.psum_scatter(done, 'ep', scatter_dimension=0, tiled=True)]
    all_gather x0 -> x1, waiting for transfers between devices: none -> 57.1 us  [experts_part(): rows = lax.all_gather(tokens, 'ep', axis=0, tiled=True)]
    reshape x6 -> x0, local copies, waits for them, and re-layouts: 28.1 us -> none  [the longest x1 7.45 us: experts_part(): grouped = back.reshape(experts, SPLIT, capacity, width)]
    reduce_sum x3 -> x1, other arithmetic: 18.6 us -> 0.71 us  [experts_part(): jnp.sum(jnp.where(expert_ids[:, :, None] == jnp.arange(experts, dtype=jnp...]
    gather x1 -> x0, local copies, waits for them, and re-layouts: 17.5 us -> none  [experts_part(): picked = grouped[flat, :, slot]]
    scatter x1 -> x0, local copies, waits for them, and re-layouts: 5.57 us -> none  [experts_part(): jnp.zeros((experts * capacity, width), jnp.bfloat16).at[target]]
  transfers between devices with their start and end apart: 2 -> 4, of which waited for: 0 -> 4; matrix products, arithmetic and copies ran while one was open for 2% -> 14% of each run, Pallas kernels for 0% -> 0%
where the time goes in v1:
time: 223 us
  waiting for transfers between devices  159 us (71%)
  matrix products  26.3 us (12%)
  between operations  15.2 us (7%)
  blocking collectives  9.81 us (4%)
  starting transfers between devices  7.5 us (3%)
  local copies, waits for them, and re-layouts  2.81 us (1%)
    reduce_scatter x1, waiting for transfers between devices, experts_part(): return lax.psum_scatter(done, 'ep', scatter_dimension=0, tiled=True)  90.7 us
    all_gather x1, waiting for transfers between devices, experts_part(): rows = lax.all_gather(tokens, 'ep', axis=0, tiled=True)  57.1 us
    dot_general x1, matrix products, experts_part(): done = jnp.dot(hidden, w_down, preferred_element_type=jnp.float32)  14.4 us
    unnamed x1, blocking collectives  9.81 us
    all_to_all x1, starting transfers between devices, experts_part(): lax.all_to_all(jnp.repeat(flat.T, SPLIT, axis=0), 'ep', split_axis=0, con...  7.39 us
    dot_general x1, matrix products, experts_part(): gate = jnp.dot(rows, w_gate, preferred_element_type=jnp.float32)  7.28 us
    all_to_all x1, waiting for transfers between devices, experts_part(): lax.all_to_all(jnp.repeat(flat.T, SPLIT, axis=0), 'ep', split_axis=0, con...  5.53 us
    all_gather x1, waiting for transfers between devices, decode_part(): latent_rows = lax.all_gather(prefill_latent, 'ep', axis=0, tiled=True)  4.6 us
  transfers between devices with their start and end apart: 4, of which 4 were waited for; matrix products, arithmetic and copies ran while one was open for 14% of the time, Pallas kernels for 0%

profile of v1, /device:TPU:0, one launch (start us, length us, event | category | flops | bytes accessed | tf_op | source)
XLA Modules:
  0.0 222.7 jit_solution(16684410003623627367)
XLA Ops:
  7.2 0.7 all-gather.3.cloned.1.call-update
  7.9 0.7 select_reduce_fusion.2
  8.6 0.6 broadcast_in_dim.67
  9.2 7.4 %all-to-all-start = ((f32[16,1,64]{2,1,0:T(1,128)}), f32[16,1,64]{2,1,0:T(1,128)S(1)}, u32[]{:S(2)}, u32[]{:S(2)}) async-start(f32[16,1,64]{2,1,0:T(1,128)} %bitcast.1), calls=%async_computation | async-start | bytes 16384 | tf_op jit(solution)/shard_map/all_to_all | solution.py:27
  16.7 0.7 all-gather.5.cloned.1.call-update
  17.4 5.5 %all-to-all-done = f32[16,1,64]{2,1,0:T(1,128)S(1)} async-done(((f32[16,1,64]{2,1,0:T(1,128)}), f32[16,1,64]{2,1,0:T(1,128)S(1)}, u32[]{:S(2)}, u32[]{:S(2)}) %all-to-all-start) | async-done | bytes 4128 | tf_op jit(solution)/shard_map/all_to_all | solution.py:27
  23.0 0.5 broadcast.48
  23.5 0.7 reduce.11
  24.2 57.1 %all-gather.3.cloned.1.call-done = bf16[1024,3584]{1,0:T(8,128)(2,1)} async-done(((bf16[64,3584]{1,0:T(8,128)(2,1)}), bf16[1024,3584]{1,0:T(8,128)(2,1)}) %all-gather.3.cloned.1.call-update) | async-done | bytes 7340048 | tf_op jit(solution)/shard_map/all_gather | solution.py:26
  81.3 7.3 %fusion.24 = f32[1024,512]{1,0:T(8,128)S(1)} fusion(bf16[1024,3584]{1,0:T(8,128)(2,1)} %all-gather.3.cloned.1.call-done, bf16[3584,512]{1,0:T(8,128)(2,1)} %param.14), kind=kOutput, calls=%fused_computation.38 | convolution fusion | flops 3758096384 | bytes 13107200 | tf_op jit(solution)/shard_map/dot_general | solution.py:30
  88.6 14.4 %multiply_convert_fusion = bf16[1024,3584]{1,0:T(8,128)(2,1)} fusion(bf16[512,3584]{1,0:T(8,128)(2,1)} %param.16, f32[1024]{0:T(1024)S(1)} %mul.51, f32[1024,512]{1,0:T(8,128)S(1)} %fusion.24, bf16[1024,3584]{1,0:T(8,128)(2,1)} %all-gather.3.cloned.1.call-done, bf16[3584,512]{1,0:T(8,128)(2,1)} %param.15), kind=kOutput, calls=%fused_computation | convolution fusion | flops 7526678528 | bytes 24121344 | tf_op jit(solution)/shard_map/dot_general | solution.py:33
  103.0 0.6 copy-done.3
  103.6 0.6 dynamic-slice
  104.9 0.2 dynamic-update-slice
  105.1 9.8 %all-reduce = s32[64]{0:T(128)S(1)} all-reduce(s32[64]{0:T(128)S(1)} %dynamic-update-slice), channel_id=1, replica_groups=mesh['group'=2,'ep'=16] {'ep'}, use_global_device_ids=true, to_apply=%add | all-reduce | flops 64 | bytes 512
  115.0 0.1 eq.36
  115.8 0.3 select_reduce_fusion.1
  116.1 0.2 fusion.15
  116.3 4.6 %all-gather.5.cloned.1.call-done = bf16[1024,576]{1,0:T(8,128)(2,1)} async-done(((bf16[64,576]{1,0:T(8,128)(2,1)}), bf16[1024,576]{1,0:T(8,128)(2,1)}) %all-gather.5.cloned.1.call-update) | async-done | bytes 1179664 | tf_op jit(solution)/shard_map/all_gather | solution.py:57
  120.9 1.9 select_reduce_fusion
  122.8 0.2 fusion.7
  123.1 0.2 convolution_multiply_fusion.1
  123.3 2.2 fusion.2
  125.5 90.7 %reduce-scatter.2.cloned.1.call-done = bf16[64,3584]{1,0:T(8,128)(2,1)} async-done(((bf16[1024,3584]{1,0:T(8,128)(2,1)}), bf16[64,3584]{1,0:T(8,128)(2,1)}) %reduce-scatter.2.cloned.1.call-update) | async-done | bytes 458768 | tf_op jit(solution)/shard_map/reduce_scatter | solution.py:35
  (18 shorter events, 0.3 us)
Async XLA Ops:
  7.2 108.6 %copy-start = (bf16[1,64,576]{2,1,0:T(8,128)(2,1)S(1)}, bf16[1,64,576]{2,1,0:T(8,128)(2,1)}, u32[]{:S(2)}) copy-start(bf16[1,64,576]{2,1,0:T(8,128)(2,1)} %param.19) | copy-start | bytes 221188
  7.2 74.1 %all-gather.3.cloned.1.call-start = ((), (), s32[]{:S(2)}) async-start(), calls=%async_computation.2 | async-start | bytes 7798784 | tf_op jit(solution)/shard_map/all_gather | solution.py:26
  9.2 13.7 %all-to-all-start = ((f32[16,1,64]{2,1,0:T(1,128)}), f32[16,1,64]{2,1,0:T(1,128)S(1)}, u32[]{:S(2)}, u32[]{:S(2)}) async-start(f32[16,1,64]{2,1,0:T(1,128)} %bitcast.1), calls=%async_computation | async-start | bytes 16384 | tf_op jit(solution)/shard_map/all_to_all | solution.py:27
  16.6 104.3 %all-gather.5.cloned.1.call-start = ((), (), s32[]{:S(2)}) async-start(), calls=%async_computation.4 | async-start | bytes 1392640 | tf_op jit(solution)/shard_map/all_gather | solution.py:57
  17.4 198.8 %reduce-scatter.2.cloned.1.call-start = ((), (), s32[]{:S(2)}) async-start(), calls=%async_computation.3 | async-start | bytes 7798784 | tf_op jit(solution)/shard_map/reduce_scatter | solution.py:35
  103.0 0.7 copy-start.3
  103.0 1.9 copy-start.2
  103.0 12.8 %copy-start.1 = (bf16[1,256,576]{1,2,0:T(8,128)(2,1)S(1)}, bf16[1,256,576]{1,2,0:T(8,128)(2,1)}, u32[]{:S(2)}) copy-start(bf16[1,256,576]{1,2,0:T(8,128)(2,1)} %param.20) | copy-start | bytes 884740
Sparse Core Ops, SparseCore 0:
  10.3 70.9 all-gather.2
  83.6 37.2 all-gather.4
  125.4 90.6 reduce-scatter.1

commit v2 on v1

--- a/solution.py
+++ b/solution.py
@@ -1,6 +1,8 @@
 import jax
 import jax.numpy as jnp
 from jax import lax
+from jax.experimental import pallas as pl
+from jax.experimental.pallas import tpu as pltpu
 from jax.sharding import PartitionSpec as P
 
 SPLIT = 2
@@ -77,7 +79,360 @@
     return (summed / new_total[:, :, None]).astype(jnp.bfloat16)
 
 
+PLANES = 4
+CHUNKS = 4
+CONTRACT_LAST = (((1,), (1,)), ((), ()))
+BF16, F32 = jnp.bfloat16, jnp.float32
+
+
+def fused_kernel(
+    tok_ref, ids_ref, gw_ref, wg_hbm, wu_hbm, wd_hbm, lat_ref, page_ref, q_ref, cache_ref, len_ref,
+    moe_ref, attn_ref,
+    xg, wg, wu, wd, hid, part, from_sib, to_y, from_y, to_z, from_z,
+    w_sem, ag_send, ag_recv, sib_send, sib_recv, y_send, y_recv, z_send, z_recv,
+):
+    me = lax.axis_index("ep")
+    z, y, c = me // 4, (me // 2) % 2, me % 2
+    expert = me // 2
+    rows, width = tok_ref.shape
+    keys = lat_ref.shape[1]
+    plane_rows = 4 * rows
+    ffw = wg.shape[1]
+    cols = width // CHUNKS
+    sib = z * 4 + y * 2 + (1 - c)
+    across = z * 4 + (1 - y) * 2 + c
+    above, below = me + 4, me - 4
+    upper = z // 2
+    near = z * (1 - upper) + (PLANES - 1 - z) * upper
+    is_end = near == 0
+    is_inner = near == 1
+
+    def plane_of(s):
+        q = jnp.where(s == 0, near, jnp.where(s == 1, 1 - near, s))
+        return q * (1 - upper) + (PLANES - 1 - q) * upper
+
+    def row_at(block):
+        return pl.ds(pl.multiple_of(block * rows, rows), rows)
+
+    def at_plane(p):
+        return pl.ds(pl.multiple_of(p * plane_rows, plane_rows), plane_rows)
+
+    def remote(src, dst, send, recv, to):
+        return pltpu.make_async_remote_copy(
+            src_ref=src, dst_ref=dst, send_sem=send, recv_sem=recv,
+            device_id={"ep": to}, device_id_type=pl.DeviceIdType.MESH,
+        )
+
+    def gather_copy(block, route, p, to):
+        return remote(xg.at[row_at(block)], xg.at[row_at(block)], ag_send.at[route, p], ag_recv.at[block], to)
+
+    loads = [
+        pltpu.make_async_copy(wg_hbm, wg, w_sem.at[0]),
+        pltpu.make_async_copy(wu_hbm, wu, w_sem.at[1]),
+        pltpu.make_async_copy(wd_hbm, wd, w_sem.at[2]),
+    ]
+    for load in loads:
+        load.start()
+
+    barrier = pltpu.get_barrier_semaphore()
+    for to in (sib, across):
+        pl.semaphore_signal(barrier, inc=1, device_id={"ep": to}, device_id_type=pl.DeviceIdType.MESH)
+
+    @pl.when(z < PLANES - 1)
+    def _():
+        pl.semaphore_signal(barrier, inc=1, device_id={"ep": above}, device_id_type=pl.DeviceIdType.MESH)
+
+    @pl.when(z > 0)
+    def _():
+        pl.semaphore_signal(barrier, inc=1, device_id={"ep": below}, device_id_type=pl.DeviceIdType.MESH)
+
+    own = row_at(me)
+    xg[own, 0:width] = tok_ref[...]
+    lane = lax.broadcasted_iota(jnp.int32, (rows, 64), 1)
+    line = lax.broadcasted_iota(jnp.int32, (rows, 64), 0)
+    ids, gw = ids_ref[...], gw_ref[...]
+    dense = jnp.zeros((rows, 64), F32)
+    for k in range(ids.shape[1]):
+        dense = dense + jnp.where(lane % 8 == ids[:, k : k + 1], gw[:, k : k + 1], 0.0)
+    high = dense.astype(BF16).astype(F32)
+    mid = (dense - high).astype(BF16).astype(F32)
+    low = dense - high - mid
+    target = jnp.zeros((rows, 64), F32)
+    for j in range(rows // PAGE):
+        target = target + jnp.where(line // PAGE == j, page_ref[j].astype(F32), 0.0)
+    extra = jnp.where(
+        lane < 8, high, jnp.where(lane < 16, mid, jnp.where(lane < 24, low, jnp.where(lane == 24, target, 0.0)))
+    )
+    xg[own, width : width + LAT] = lat_ref[:, :LAT]
+    xg[own, width + LAT :] = jnp.concatenate([lat_ref[:, LAT:].astype(F32), extra], axis=1).astype(BF16)
+
+    pl.semaphore_wait(barrier, 3 + jnp.where(is_inner, 1, 0))
+
+    def arrive(s):
+        p = plane_of(s)
+        block = p * 4 + y * 2 + c
+        if s > 0:
+            gather_copy(block, 0, p, sib).wait_recv()
+
+        @pl.when((p <= z) & (z < PLANES - 1))
+        def _():
+            gather_copy(block, 0, p, above).start()
+
+        @pl.when((p >= z) & (z > 0))
+        def _():
+            gather_copy(block, 1, p, below).start()
+
+        gather_copy(block, 2, p, across).start()
+        gather_copy(block, 3, p, sib).start()
+
+    def sib_copy(p, side, ch, core):
+        block = p * 4 + side * 2 + core
+        at = pl.ds(pl.multiple_of(ch * cols, 128), cols)
+        return remote(
+            part.at[row_at(block), at], from_sib.at[row_at(p * 2 + side), at],
+            sib_send.at[side, p, ch], sib_recv.at[side, p, ch], sib,
+        )
+
+    def y_copy(p, ch):
+        at = pl.ds(pl.multiple_of(ch * cols, 128), cols)
+        return remote(to_y.at[row_at(p), at], from_y.at[row_at(p), at], y_send.at[p, ch], y_recv.at[p, ch], across)
+
+    def z_copy(p, ch, way, to):
+        at = pl.ds(pl.multiple_of(ch * cols, 128), cols)
+        return remote(
+            to_z.at[row_at(p), at], from_z.at[way, row_at(p), at], z_send.at[p, ch], z_recv.at[way, p, ch], to
+        )
+
+    def experts_on(p):
+        at = at_plane(p)
+
+        @pl.loop(0, ffw // 256)
+        def _(f):
+            fs = pl.ds(pl.multiple_of(f * 256, 256), 256)
+            gate = jnp.dot(xg[at, 0:width], wg[:, fs], preferred_element_type=F32)
+            upward = jnp.dot(xg[at, 0:width], wu[:, fs], preferred_element_type=F32)
+            hid[:, fs] = (gate / (1.0 + jnp.exp(-gate)) * upward).astype(BF16)
+
+        tile = xg[at, width + LAT :].astype(F32)
+        spot = lax.broadcasted_iota(jnp.int32, tile.shape, 1) - 64
+        chosen = (spot >= 0) & (spot < 24) & (spot % 8 == expert)
+        scale = jnp.sum(jnp.where(chosen, tile, 0.0), axis=1, keepdims=True)
+
+        @pl.loop(0, CHUNKS)
+        def _(ch):
+            cs = pl.ds(pl.multiple_of(ch * cols, 128), cols)
+            out = jnp.dot(hid[...], wd[:, cs], preferred_element_type=F32)
+            part[at, cs] = (out * scale).astype(BF16)
+            for side in range(2):
+                sib_copy(p, side, ch, 1 - c).start()
+
+    def sum_pair(p):
+        @pl.loop(0, CHUNKS)
+        def _(ch):
+            cs = pl.ds(pl.multiple_of(ch * cols, 128), cols)
+            sib_copy(p, 0, ch, c).wait_recv()
+            sib_copy(p, 1, ch, c).wait_recv()
+            mine = part[row_at(p * 4 + (1 - y) * 2 + c), cs].astype(F32)
+            to_y[row_at(p), cs] = (mine + from_sib[row_at(p * 2 + (1 - y)), cs].astype(F32)).astype(BF16)
+            y_copy(p, ch).start()
+
+    def column_sum(p, cs):
+        total = part[row_at(p * 4 + y * 2 + c), cs].astype(F32)
+        total = total + from_sib[row_at(p * 2 + y), cs].astype(F32)
+        return total + from_y[row_at(p), cs].astype(F32)
+
+    def pass_on(p):
+        @pl.loop(0, CHUNKS)
+        def _(ch):
+            cs = pl.ds(pl.multiple_of(ch * cols, 128), cols)
+            y_copy(p, ch).wait_recv()
+
+            @pl.when(is_end)
+            def _():
+                to_z[row_at(p), cs] = column_sum(p, cs).astype(BF16)
+
+            @pl.when(is_inner)
+            def _():
+                way = jnp.where(p > z, 0, 1)
+                z_copy(p, ch, way, sib).wait_recv()
+                to_z[row_at(p), cs] = (column_sum(p, cs) + from_z[way, row_at(p), cs].astype(F32)).astype(BF16)
+
+            @pl.when(p > z)
+            def _():
+                z_copy(p, ch, 0, above).start()
+
+            @pl.when(p < z)
+            def _():
+                z_copy(p, ch, 1, below).start()
+
+    def finish():
+        @pl.loop(0, CHUNKS)
+        def _(ch):
+            cs = pl.ds(pl.multiple_of(ch * cols, 128), cols)
+            y_copy(z, ch).wait_recv()
+
+            @pl.when(z > 0)
+            def _():
+                z_copy(z, ch, 0, sib).wait_recv()
+
+            @pl.when(z < PLANES - 1)
+            def _():
+                z_copy(z, ch, 1, sib).wait_recv()
+
+            total = column_sum(z, cs)
+
+            @pl.when(is_inner)
+            def _():
+                both = from_z[0, row_at(z), cs].astype(F32) + from_z[1, row_at(z), cs].astype(F32)
+                moe_ref[:, cs] = (total + both).astype(BF16)
+
+            @pl.when(is_end)
+            def _():
+                moe_ref[:, cs] = (total + from_z[1 - upper, row_at(z), cs].astype(F32)).astype(BF16)
+
+    def attend():
+        q = q_ref[0]
+        cached = lax.dot_general(q, cache_ref[0], CONTRACT_LAST, preferred_element_type=F32) * score_scale
+        fresh = lax.dot_general(q, xg[:, width : width + keys], CONTRACT_LAST, preferred_element_type=F32)
+        fresh = fresh * score_scale
+        pick = (lax.broadcasted_iota(jnp.int32, (8, 128), 1) == 64 + 24).astype(F32).astype(BF16)
+        wanted = lax.dot_general(pick, xg[:, width + LAT :], CONTRACT_LAST, preferred_element_type=F32)[0:1, :]
+        match = jnp.abs(wanted - me.astype(F32)) < 0.5
+        valid = lax.broadcasted_iota(jnp.int32, cached.shape, 1) < len_ref[0]
+        peak = jnp.maximum(
+            jnp.max(jnp.where(valid, cached, mask_low), axis=1, keepdims=True),
+            jnp.max(jnp.where(match, fresh, mask_low), axis=1, keepdims=True),
+        )
+        w_old = jnp.where(valid, jnp.exp(cached - peak), 0.0)
+        w_new = jnp.where(match, jnp.exp(fresh - peak), 0.0)
+        total = jnp.sum(w_old, axis=1, keepdims=True) + jnp.sum(w_new, axis=1, keepdims=True)
+        summed = jnp.dot(w_old.astype(BF16), cache_ref[0, :, :LAT], preferred_element_type=F32)
+        summed = summed + jnp.dot(w_new.astype(BF16), xg[:, width : width + LAT], preferred_element_type=F32)
+        attn_ref[0] = (summed / total).astype(BF16)
+
+    arrive(0)
+
+    @pl.loop(0, PLANES)
+    def _(s):
+        @pl.when(s == 0)
+        def _():
+            arrive(1)
+
+        @pl.when((is_inner & (s == 0)) | (is_end & (s == 1)))
+        def _():
+            arrive(2)
+
+        @pl.when((is_inner & (s == 1)) | (is_end & (s == 2)))
+        def _():
+            arrive(3)
+
+        p = plane_of(s)
+        crossed = p * 4 + (1 - y) * 2 + c
+        gather_copy(crossed, 0, p, sib).wait_recv()
+        gather_copy(crossed, 4, p, sib).start()
+        gather_copy(p * 4 + y * 2 + (1 - c), 0, p, sib).wait_recv()
+        gather_copy(p * 4 + (1 - y) * 2 + (1 - c), 0, p, sib).wait_recv()
+
+        @pl.when(s == 0)
+        def _():
+            for load in loads:
+                load.wait()
+
+        experts_on(p)
+        sum_pair(p)
+
+        @pl.when(is_end & (s == 2))
+        def _():
+            pass_on(plane_of(1))
+
+    attend()
+    pass_on(plane_of(2))
+    pass_on(plane_of(3))
+
+    @pl.when(is_inner)
+    def _():
+        pass_on(plane_of(1))
+
+    finish()
+
+    @pl.loop(0, PLANES)
+    def _(p):
+        block = p * 4 + y * 2 + c
+
+        @pl.when((p <= z) & (z < PLANES - 1))
+        def _():
+            gather_copy(block, 0, p, above).wait_send()
+
+        @pl.when((p >= z) & (z > 0))
+        def _():
+            gather_copy(block, 1, p, below).wait_send()
+
+        gather_copy(block, 2, p, across).wait_send()
+        gather_copy(block, 3, p, sib).wait_send()
+        gather_copy(p * 4 + (1 - y) * 2 + c, 4, p, sib).wait_send()
+
+        @pl.loop(0, CHUNKS)
+        def _(ch):
+            for side in range(2):
+                sib_copy(p, side, ch, 1 - c).wait_send()
+            y_copy(p, ch).wait_send()
+
+            @pl.when(p != z)
+            def _():
+                z_copy(p, ch, 0, sib).wait_send()
+
+
+def fused(tokens, expert_ids, gate_weights, w_gate, w_up, w_down, prefill_latent, page_target, queries, cache_latent, cache_len):
+    rows, width = tokens.shape
+    keys = prefill_latent.shape[1]
+    ffw = w_gate.shape[1]
+    count = lax.axis_size("ep")
+    vmem = pl.BlockSpec(memory_space=pltpu.VMEM)
+    smem = pl.BlockSpec(memory_space=pltpu.SMEM)
+    hbm = pl.BlockSpec(memory_space=pl.ANY)
+    dma = pltpu.SemaphoreType.DMA
+    return pl.pallas_call(
+        fused_kernel,
+        out_shape=(
+            jax.ShapeDtypeStruct((rows, width), BF16),
+            jax.ShapeDtypeStruct((1, queries.shape[1], LAT), BF16),
+        ),
+        in_specs=[vmem, vmem, vmem, hbm, hbm, hbm, vmem, smem, vmem, vmem, smem],
+        out_specs=(vmem, vmem),
+        scratch_shapes=[
+            pltpu.VMEM((count * rows, width + keys + 64), BF16),
+            pltpu.VMEM((width, ffw), BF16),
+            pltpu.VMEM((width, ffw), BF16),
+            pltpu.VMEM((ffw, width), BF16),
+            pltpu.VMEM((4 * rows, ffw), BF16),
+            pltpu.VMEM((count * rows, width), BF16),
+            pltpu.VMEM((count // 2 * rows, width), BF16),
+            pltpu.VMEM((PLANES * rows, width), BF16),
+            pltpu.VMEM((PLANES * rows, width), BF16),
+            pltpu.VMEM((PLANES * rows, width), BF16),
+            pltpu.VMEM((2, PLANES * rows, width), BF16),
+            dma((3,)),
+            dma((5, PLANES)),
+            dma((count,)),
+            dma((2, PLANES, CHUNKS)),
+            dma((2, PLANES, CHUNKS)),
+            dma((PLANES, CHUNKS)),
+            dma((PLANES, CHUNKS)),
+            dma((PLANES, CHUNKS)),
+            dma((2, PLANES, CHUNKS)),
+        ],
+        compiler_params=pltpu.CompilerParams(
+            collective_id=0, has_side_effects=True, vmem_limit_bytes=60 * 1024 * 1024
+        ),
+    )(tokens, expert_ids, gate_weights, w_gate, w_up, w_down, prefill_latent, page_target, queries, cache_latent, cache_len)
+
+
 def local(tokens, expert_ids, gate_weights, w_gate, w_up, w_down, prefill_latent, page_target, queries, cache_latent, cache_len):
+    if lax.axis_size("ep") == 16 and queries.shape[0] == 1:
+        return fused(
+            tokens, expert_ids, gate_weights, w_gate, w_up, w_down,
+            prefill_latent, page_target, queries, cache_latent, cache_len,
+        )
     moe_out = experts_part(tokens, expert_ids, gate_weights, w_gate, w_up, w_down)
     attn_out = decode_part(prefill_latent, page_target, queries, cache_latent, cache_len)
     return (moe_out, attn_out)

time: 223 us -> 127 us (0.57)
  waiting for transfers between devices: 159 us -> 0 us
  Pallas kernels: 0 us -> 117 us
  matrix products: 26.3 us -> 0 us
  between operations: 15.2 us -> 1.29 us
  blocking collectives: 9.81 us -> 0 us
  starting transfers between devices: 7.5 us -> 0 us
  local copies, waits for them, and re-layouts: 2.81 us -> 7.91 us
    pallas_call x0 -> x1, Pallas kernels: none -> 117 us  [fused(): pl.pallas_call(fused_kernel, out_shape=(jax.ShapeDtypeStruct((rows, width...]
    reduce_scatter x1 -> x0, waiting for transfers between devices: 90.7 us -> none  [experts_part(): return lax.psum_scatter(done, 'ep', scatter_dimension=0, tiled=True)]
    all_gather x2 -> x0, waiting for transfers between devices: 61.7 us -> none  [the longest x1 57.1 us: experts_part(): rows = lax.all_gather(tokens, 'ep', axis=0, tiled=True)]
    dot_general x6 -> x0, matrix products: 26.3 us -> none  [the longest x1 14.4 us: experts_part(): done = jnp.dot(hidden, w_down, preferred_element_type=jnp.float32)]
    unnamed x1 -> x0, blocking collectives: 9.81 us -> none
    all_to_all x1 -> x0, starting transfers between devices: 7.39 us -> none  [experts_part(): lax.all_to_all(jnp.repeat(flat.T, SPLIT, axis=0), 'ep', split_axis=0, con...]
    unnamed x11 -> x5, local copies, waits for them, and re-layouts: 1.46 us -> 7.91 us
    all_to_all x1 -> x0, waiting for transfers between devices: 5.53 us -> none  [experts_part(): lax.all_to_all(jnp.repeat(flat.T, SPLIT, axis=0), 'ep', split_axis=0, con...]
  transfers between devices with their start and end apart: 4 -> 0, of which waited for: 4 -> 0; matrix products, arithmetic and copies ran while one was open for 14% -> 0% of each run, Pallas kernels for 0% -> 0%
where the time goes in v2:
time: 127 us
  Pallas kernels  117 us (92%)
  local copies, waits for them, and re-layouts  7.91 us (6%)
  between operations  1.29 us (1%)
    pallas_call x1, Pallas kernels, fused(): pl.pallas_call(fused_kernel, out_shape=(jax.ShapeDtypeStruct((rows, width...  117 us
    unnamed x5, local copies, waits for them, and re-layouts  7.91 us

profile of v2, /device:TPU:0, one launch (start us, length us, event | category | flops | bytes accessed | tf_op | source)
XLA Modules:
  0.0 126.7 jit_solution(11785004663562192306)
XLA Ops:
  1.3 1.4 %copy.13.ids_ref = s32[64,4]{1,0:T(8,128)} copy(s32[64,4]{0,1:T(4,128)} %param.12) | data formatting | bytes 2048 | tf_op args[1]
  2.7 1.4 %copy.14.gw_ref = f32[64,4]{1,0:T(8,128)} copy(f32[64,4]{0,1:T(4,128)} %param.13) | data formatting | bytes 2048 | tf_op args[2]
  4.0 1.9 %copy.15.cache_ref = bf16[1,256,576]{2,1,0:T(8,128)(2,1)} copy(bf16[1,256,576]{1,2,0:T(8,128)(2,1)} %param.20) | data formatting | bytes 589824 | tf_op args[9]
  5.9 117.5 %shard_map.122 = (bf16[64,3584]{1,0:T(8,128)(2,1)}, bf16[1,64,512]{2,1,0:T(8,128)(2,1)}) custom-call(bf16[64,3584]{1,0:T(8,128)(2,1)} %tok_ref.1, s32[64,4]{1,0:T(8,128)} %copy.13.ids_ref, f32[64,4]{1,0:T(8,128)} %copy.14.gw_ref, bf16[3584,512]{1,0:T(8,128)(2,1)} %wg_hbm.1, bf16[3584,512]{1,0:T(8,128)(2,1)} %wu_hbm.1, bf16[512,3584]{1,0:T(8,128)(2,1)} %wd_hbm.1, ...), custom_call_target="tpu_custom_call" | custom-call | tf_op jit(solution)/shard_map/pallas_call | solution.py:394
  123.4 1.8 %copy.19 = bf16[64,3584]{1,0:T(8,128)(2,1)} copy(bf16[64,3584]{1,0:T(8,128)(2,1)} %get-tuple-element.4) | data formatting | bytes 917504
  125.2 1.5 %copy.20 = bf16[1,64,512]{2,1,0:T(8,128)(2,1)} copy(bf16[1,64,512]{2,1,0:T(8,128)(2,1)} %get-tuple-element.5) | data formatting | bytes 131072

commit v3 on v2

--- a/solution.py
+++ b/solution.py
@@ -88,8 +88,8 @@
 def fused_kernel(
     tok_ref, ids_ref, gw_ref, wg_hbm, wu_hbm, wd_hbm, lat_ref, page_ref, q_ref, cache_ref, len_ref,
     moe_ref, attn_ref,
-    xg, wg, wu, wd, hid, part, from_sib, to_y, from_y, to_z, from_z,
-    w_sem, ag_send, ag_recv, sib_send, sib_recv, y_send, y_recv, z_send, z_recv,
+    xg, wg, wu, wd, hid, part, from_sib, to_y, from_y, to_z, from_z, from_x,
+    w_sem, ag_send, ag_recv, sib_send, sib_recv, y_send, y_recv, z_send, z_recv, x_recv,
 ):
     me = lax.axis_index("ep")
     z, y, c = me // 4, (me // 2) % 2, me % 2
@@ -106,6 +106,8 @@
     near = z * (1 - upper) + (PLANES - 1 - z) * upper
     is_end = near == 0
     is_inner = near == 1
+    outward = me + 4 - 8 * upper
+    inward = me - 4 + 8 * upper
 
     def plane_of(s):
         q = jnp.where(s == 0, near, jnp.where(s == 1, 1 - near, s))
@@ -148,21 +150,25 @@
 
     own = row_at(me)
     xg[own, 0:width] = tok_ref[...]
-    lane = lax.broadcasted_iota(jnp.int32, (rows, 64), 1)
-    line = lax.broadcasted_iota(jnp.int32, (rows, 64), 0)
+    lane = lax.broadcasted_iota(jnp.int32, (64, rows), 1)
+    line = lax.broadcasted_iota(jnp.int32, (64, rows), 0)
     ids, gw = ids_ref[...], gw_ref[...]
-    dense = jnp.zeros((rows, 64), F32)
-    for k in range(ids.shape[1]):
-        dense = dense + jnp.where(lane % 8 == ids[:, k : k + 1], gw[:, k : k + 1], 0.0)
+    dense = jnp.zeros((64, rows), F32)
+    for k in range(ids.shape[0]):
+        dense = dense + jnp.where(line % 8 == ids[k : k + 1, :], gw[k : k + 1, :], 0.0)
     high = dense.astype(BF16).astype(F32)
     mid = (dense - high).astype(BF16).astype(F32)
     low = dense - high - mid
-    target = jnp.zeros((rows, 64), F32)
+    target = jnp.zeros((64, rows), F32)
     for j in range(rows // PAGE):
-        target = target + jnp.where(line // PAGE == j, page_ref[j].astype(F32), 0.0)
+        target = target + jnp.where(lane // PAGE == j, page_ref[j].astype(F32), 0.0)
     extra = jnp.where(
-        lane < 8, high, jnp.where(lane < 16, mid, jnp.where(lane < 24, low, jnp.where(lane == 24, target, 0.0)))
-    )
+        line < 8, high, jnp.where(line < 16, mid, jnp.where(line < 24, low, jnp.where(line == 24, target, 0.0)))
+    )
+    eye_lane = lax.broadcasted_iota(jnp.int32, (rows, rows), 1)
+    eye_line = lax.broadcasted_iota(jnp.int32, (rows, rows), 0)
+    eye = (eye_lane == eye_line).astype(F32).astype(BF16)
+    extra = lax.dot_general(eye, extra.astype(BF16), CONTRACT_LAST, preferred_element_type=F32)
     xg[own, width : width + LAT] = lat_ref[:, :LAT]
     xg[own, width + LAT :] = jnp.concatenate([lat_ref[:, LAT:].astype(F32), extra], axis=1).astype(BF16)
 
@@ -182,7 +188,8 @@
         def _():
             gather_copy(block, 1, p, below).start()
 
-        gather_copy(block, 2, p, across).start()
+        if s < PLANES - 1:
+            gather_copy(block, 2, p, across).start()
         gather_copy(block, 3, p, sib).start()
 
     def sib_copy(p, side, ch, core):
@@ -197,6 +204,12 @@
         at = pl.ds(pl.multiple_of(ch * cols, 128), cols)
         return remote(to_y.at[row_at(p), at], from_y.at[row_at(p), at], y_send.at[p, ch], y_recv.at[p, ch], across)
 
+    def x_copy(p, ch, slot):
+        at = pl.ds(pl.multiple_of(ch * cols, 128), cols)
+        return remote(
+            to_y.at[row_at(p), at], from_x.at[row_at(slot), at], y_send.at[p, ch], x_recv.at[slot, ch], outward
+        )
+
     def z_copy(p, ch, way, to):
         at = pl.ds(pl.multiple_of(ch * cols, 128), cols)
         return remote(
@@ -226,44 +239,87 @@
             for side in range(2):
                 sib_copy(p, side, ch, 1 - c).start()
 
-    def sum_pair(p):
+    def each_chunk(body):
         @pl.loop(0, CHUNKS)
         def _(ch):
-            cs = pl.ds(pl.multiple_of(ch * cols, 128), cols)
-            sib_copy(p, 0, ch, c).wait_recv()
-            sib_copy(p, 1, ch, c).wait_recv()
-            mine = part[row_at(p * 4 + (1 - y) * 2 + c), cs].astype(F32)
-            to_y[row_at(p), cs] = (mine + from_sib[row_at(p * 2 + (1 - y)), cs].astype(F32)).astype(BF16)
+            body(ch, pl.ds(pl.multiple_of(ch * cols, 128), cols))
+
+    def pair_in(p, ch):
+        sib_copy(p, 0, ch, c).wait_recv()
+        sib_copy(p, 1, ch, c).wait_recv()
+
+    def other_sum(p, cs):
+        mine = part[row_at(p * 4 + (1 - y) * 2 + c), cs].astype(F32)
+        return mine + from_sib[row_at(p * 2 + (1 - y)), cs].astype(F32)
+
+    def own_sum(p, cs):
+        mine = part[row_at(p * 4 + y * 2 + c), cs].astype(F32)
+        return mine + from_sib[row_at(p * 2 + y), cs].astype(F32)
+
+    def column_sum(p, cs):
+        return own_sum(p, cs) + from_y[row_at(p), cs].astype(F32)
+
+    def send_z(p, ch):
+        @pl.when(p > z)
+        def _():
+            z_copy(p, ch, 0, above).start()
+
+        @pl.when(p < z)
+        def _():
+            z_copy(p, ch, 1, below).start()
+
+    def cross(p):
+        def body(ch, cs):
+            pair_in(p, ch)
+            to_y[row_at(p), cs] = other_sum(p, cs).astype(BF16)
             y_copy(p, ch).start()
 
-    def column_sum(p, cs):
-        total = part[row_at(p * 4 + y * 2 + c), cs].astype(F32)
-        total = total + from_sib[row_at(p * 2 + y), cs].astype(F32)
-        return total + from_y[row_at(p), cs].astype(F32)
-
-    def pass_on(p):
-        @pl.loop(0, CHUNKS)
-        def _(ch):
-            cs = pl.ds(pl.multiple_of(ch * cols, 128), cols)
+        each_chunk(body)
+
+    def cross_with_far(p):
+        def body(ch, cs):
+            pair_in(p, ch)
+            x_copy(p, ch, 1).wait_recv()
+            to_y[row_at(p), cs] = (other_sum(p, cs) + from_x[row_at(1), cs].astype(F32)).astype(BF16)
+            y_copy(p, ch).start()
+
+        each_chunk(body)
+
+    def far_first(p):
+        def body(ch, cs):
+            pair_in(p, ch)
+            to_y[row_at(p), cs] = other_sum(p, cs).astype(BF16)
+            x_copy(p, ch, 0).start()
+            to_z[row_at(p), cs] = own_sum(p, cs).astype(BF16)
+            send_z(p, ch)
+
+        each_chunk(body)
+
+    def far_second(p):
+        def body(ch, cs):
+            pair_in(p, ch)
+            x_copy(p, ch, 0).wait_recv()
+            to_y[row_at(p), cs] = (other_sum(p, cs) + from_x[row_at(0), cs].astype(F32)).astype(BF16)
+            x_copy(p, ch, 1).start()
+            way = jnp.where(p > z, 0, 1)
+            z_copy(p, ch, way, sib).wait_recv()
+            to_z[row_at(p), cs] = (own_sum(p, cs) + from_z[way, row_at(p), cs].astype(F32)).astype(BF16)
+            send_z(p, ch)
+
+        each_chunk(body)
+
+    def pass_on(p, chained):
+        def body(ch, cs):
             y_copy(p, ch).wait_recv()
-
-            @pl.when(is_end)
-            def _():
-                to_z[row_at(p), cs] = column_sum(p, cs).astype(BF16)
-
-            @pl.when(is_inner)
-            def _():
+            if chained:
                 way = jnp.where(p > z, 0, 1)
                 z_copy(p, ch, way, sib).wait_recv()
                 to_z[row_at(p), cs] = (column_sum(p, cs) + from_z[way, row_at(p), cs].astype(F32)).astype(BF16)
-
-            @pl.when(p > z)
-            def _():
-                z_copy(p, ch, 0, above).start()
-
-            @pl.when(p < z)
-            def _():
-                z_copy(p, ch, 1, below).start()
+            else:
+                to_z[row_at(p), cs] = column_sum(p, cs).astype(BF16)
+            send_z(p, ch)
+
+        each_chunk(body)
 
     def finish():
         @pl.loop(0, CHUNKS)
@@ -292,7 +348,7 @@
 
     def attend():
         q = q_ref[0]
-        cached = lax.dot_general(q, cache_ref[0], CONTRACT_LAST, preferred_element_type=F32) * score_scale
+        cached = jnp.dot(q, cache_ref[0], preferred_element_type=F32) * score_scale
         fresh = lax.dot_general(q, xg[:, width : width + keys], CONTRACT_LAST, preferred_element_type=F32)
         fresh = fresh * score_scale
         pick = (lax.broadcasted_iota(jnp.int32, (8, 128), 1) == 64 + 24).astype(F32).astype(BF16)
@@ -306,7 +362,7 @@
         w_old = jnp.where(valid, jnp.exp(cached - peak), 0.0)
         w_new = jnp.where(match, jnp.exp(fresh - peak), 0.0)
         total = jnp.sum(w_old, axis=1, keepdims=True) + jnp.sum(w_new, axis=1, keepdims=True)
-        summed = jnp.dot(w_old.astype(BF16), cache_ref[0, :, :LAT], preferred_element_type=F32)
+        summed = lax.dot_general(w_old.astype(BF16), cache_ref[0, :LAT, :], CONTRACT_LAST, preferred_element_type=F32)
         summed = summed + jnp.dot(w_new.astype(BF16), xg[:, width : width + LAT], preferred_element_type=F32)
         attn_ref[0] = (summed / total).astype(BF16)
 
@@ -325,11 +381,24 @@
         @pl.when((is_inner & (s == 1)) | (is_end & (s == 2)))
         def _():
             arrive(3)
+
+        @pl.when(is_end & (s == 3))
+        def _():
+            pass_on(plane_of(2), False)
 
         p = plane_of(s)
         crossed = p * 4 + (1 - y) * 2 + c
         gather_copy(crossed, 0, p, sib).wait_recv()
         gather_copy(crossed, 4, p, sib).start()
+
+        @pl.when(is_inner & (s == 1))
+        def _():
+            gather_copy(crossed, 5, p, outward).start()
+
+        @pl.when(is_inner & (s == 3))
+        def _():
+            gather_copy(crossed, 5, p, inward).start()
+
         gather_copy(p * 4 + y * 2 + (1 - c), 0, p, sib).wait_recv()
         gather_copy(p * 4 + (1 - y) * 2 + (1 - c), 0, p, sib).wait_recv()
 
@@ -339,19 +408,27 @@
                 load.wait()
 
         experts_on(p)
-        sum_pair(p)
+
+        @pl.when((s == 0) | (s == 2) | (is_end & (s == 1)))
+        def _():
+            cross(p)
 
         @pl.when(is_end & (s == 2))
         def _():
-            pass_on(plane_of(1))
+            pass_on(plane_of(1), False)
+
+        @pl.when(is_end & (s == 3))
+        def _():
+            far_first(p)
 
     attend()
-    pass_on(plane_of(2))
-    pass_on(plane_of(3))
 
     @pl.when(is_inner)
     def _():
-        pass_on(plane_of(1))
+        far_second(plane_of(3))
+        pass_on(plane_of(2), True)
+        cross_with_far(plane_of(1))
+        pass_on(plane_of(1), True)
 
     finish()
 
@@ -367,7 +444,14 @@
         def _():
             gather_copy(block, 1, p, below).wait_send()
 
-        gather_copy(block, 2, p, across).wait_send()
+        @pl.when(p != plane_of(3))
+        def _():
+            gather_copy(block, 2, p, across).wait_send()
+
+        @pl.when(is_inner & ((p == plane_of(1)) | (p == plane_of(3))))
+        def _():
+            gather_copy(p * 4 + (1 - y) * 2 + c, 5, p, sib).wait_send()
+
         gather_copy(block, 3, p, sib).wait_send()
         gather_copy(p * 4 + (1 - y) * 2 + c, 4, p, sib).wait_send()
 
@@ -411,8 +495,9 @@
             pltpu.VMEM((PLANES * rows, width), BF16),
             pltpu.VMEM((PLANES * rows, width), BF16),
             pltpu.VMEM((2, PLANES * rows, width), BF16),
+            pltpu.VMEM((2 * rows, width), BF16),
             dma((3,)),
-            dma((5, PLANES)),
+            dma((6, PLANES)),
             dma((count,)),
             dma((2, PLANES, CHUNKS)),
             dma((2, PLANES, CHUNKS)),
@@ -420,11 +505,15 @@
             dma((PLANES, CHUNKS)),
             dma((PLANES, CHUNKS)),
             dma((2, PLANES, CHUNKS)),
+            dma((2, CHUNKS)),
         ],
         compiler_params=pltpu.CompilerParams(
             collective_id=0, has_side_effects=True, vmem_limit_bytes=60 * 1024 * 1024
         ),
-    )(tokens, expert_ids, gate_weights, w_gate, w_up, w_down, prefill_latent, page_target, queries, cache_latent, cache_len)
+    )(
+        tokens, expert_ids.T, gate_weights.T, w_gate, w_up, w_down, prefill_latent, page_target,
+        queries, jnp.swapaxes(cache_latent, 1, 2), cache_len,
+    )
 
 
 def local(tokens, expert_ids, gate_weights, w_gate, w_up, w_down, prefill_latent, page_target, queries, cache_latent, cache_len):

time: 127 us -> 124 us (0.976)
  local copies, waits for them, and re-layouts: 7.91 us -> 3.29 us
  Pallas kernels: 117 us -> 120 us
    unnamed x5 -> x2, local copies, waits for them, and re-layouts: 7.91 us -> 3.29 us
    pallas_call x1, Pallas kernels: 117 us -> 120 us  [fused(): pl.pallas_call(fused_kernel, out_shape=(jax.ShapeDtypeStruct((rows, width...]
where the time goes in v3:
time: 124 us
  Pallas kernels  120 us (97%)
  local copies, waits for them, and re-layouts  3.29 us (3%)
  between operations  1.29 us (1%)
    pallas_call x1, Pallas kernels, fused(): pl.pallas_call(fused_kernel, out_shape=(jax.ShapeDtypeStruct((rows, width...  120 us
    unnamed x2, local copies, waits for them, and re-layouts  3.29 us

profile of v3, /device:TPU:0, one launch (start us, length us, event | category | flops | bytes accessed | tf_op | source)
XLA Modules:
  0.0 124.1 jit_solution(3092231538414850949)
XLA Ops:
  1.3 119.5 %shard_map.122 = (bf16[64,3584]{1,0:T(8,128)(2,1)}, bf16[1,64,512]{2,1,0:T(8,128)(2,1)}) custom-call(bf16[64,3584]{1,0:T(8,128)(2,1)} %tok_ref.1, s32[4,64]{1,0:T(4,128)} %bitcast.4, f32[4,64]{1,0:T(4,128)} %bitcast.5, bf16[3584,512]{1,0:T(8,128)(2,1)} %wg_hbm.1, bf16[3584,512]{1,0:T(8,128)(2,1)} %wu_hbm.1, bf16[512,3584]{1,0:T(8,128)(2,1)} %wd_hbm.1, ...), custom_call_target="tpu_custom_call" | custom-call | tf_op jit(solution)/shard_map/pallas_call | solution.py:478
  120.8 1.8 %copy.16 = bf16[64,3584]{1,0:T(8,128)(2,1)} copy(bf16[64,3584]{1,0:T(8,128)(2,1)} %get-tuple-element.4) | data formatting | bytes 917504
  122.6 1.5 %copy.17 = bf16[1,64,512]{2,1,0:T(8,128)(2,1)} copy(bf16[1,64,512]{2,1,0:T(8,128)(2,1)} %get-tuple-element.5) | data formatting | bytes 131072

commit v4 on v3

--- a/solution.py
+++ b/solution.py
@@ -88,8 +88,8 @@
 def fused_kernel(
     tok_ref, ids_ref, gw_ref, wg_hbm, wu_hbm, wd_hbm, lat_ref, page_ref, q_ref, cache_ref, len_ref,
     moe_ref, attn_ref,
-    xg, wg, wu, wd, hid, part, from_sib, to_y, from_y, to_z, from_z, from_x,
-    w_sem, ag_send, ag_recv, sib_send, sib_recv, y_send, y_recv, z_send, z_recv, x_recv,
+    xg, wg, wu, wd, hid, part, from_sib, to_y, from_y, to_z, from_z,
+    w_sem, ag_send, ag_recv, sib_send, sib_recv, y_send, y_recv, z_send, z_recv,
 ):
     me = lax.axis_index("ep")
     z, y, c = me // 4, (me // 2) % 2, me % 2
@@ -204,12 +204,6 @@
         at = pl.ds(pl.multiple_of(ch * cols, 128), cols)
         return remote(to_y.at[row_at(p), at], from_y.at[row_at(p), at], y_send.at[p, ch], y_recv.at[p, ch], across)
 
-    def x_copy(p, ch, slot):
-        at = pl.ds(pl.multiple_of(ch * cols, 128), cols)
-        return remote(
-            to_y.at[row_at(p), at], from_x.at[row_at(slot), at], y_send.at[p, ch], x_recv.at[slot, ch], outward
-        )
-
     def z_copy(p, ch, way, to):
         at = pl.ds(pl.multiple_of(ch * cols, 128), cols)
         return remote(
@@ -273,38 +267,6 @@
             pair_in(p, ch)
             to_y[row_at(p), cs] = other_sum(p, cs).astype(BF16)
             y_copy(p, ch).start()
-
-        each_chunk(body)
-
-    def cross_with_far(p):
-        def body(ch, cs):
-            pair_in(p, ch)
-            x_copy(p, ch, 1).wait_recv()
-            to_y[row_at(p), cs] = (other_sum(p, cs) + from_x[row_at(1), cs].astype(F32)).astype(BF16)
-            y_copy(p, ch).start()
-
-        each_chunk(body)
-
-    def far_first(p):
-        def body(ch, cs):
-            pair_in(p, ch)
-            to_y[row_at(p), cs] = other_sum(p, cs).astype(BF16)
-            x_copy(p, ch, 0).start()
-            to_z[row_at(p), cs] = own_sum(p, cs).astype(BF16)
-            send_z(p, ch)
-
-        each_chunk(body)
-
-    def far_second(p):
-        def body(ch, cs):
-            pair_in(p, ch)
-            x_copy(p, ch, 0).wait_recv()
-            to_y[row_at(p), cs] = (other_sum(p, cs) + from_x[row_at(0), cs].astype(F32)).astype(BF16)
-            x_copy(p, ch, 1).start()
-            way = jnp.where(p > z, 0, 1)
-            z_copy(p, ch, way, sib).wait_recv()
-            to_z[row_at(p), cs] = (own_sum(p, cs) + from_z[way, row_at(p), cs].astype(F32)).astype(BF16)
-            send_z(p, ch)
 
         each_chunk(body)
 
@@ -409,25 +371,22 @@
 
         experts_on(p)
 
-        @pl.when((s == 0) | (s == 2) | (is_end & (s == 1)))
-        def _():
-            cross(p)
+        cross(p)
 
         @pl.when(is_end & (s == 2))
         def _():
             pass_on(plane_of(1), False)
 
-        @pl.when(is_end & (s == 3))
-        def _():
-            far_first(p)
-
     attend()
+
+    @pl.when(is_end)
+    def _():
+        pass_on(plane_of(3), False)
 
     @pl.when(is_inner)
     def _():
-        far_second(plane_of(3))
         pass_on(plane_of(2), True)
-        cross_with_far(plane_of(1))
+        pass_on(plane_of(3), True)
         pass_on(plane_of(1), True)
 
     finish()
@@ -495,7 +454,6 @@
             pltpu.VMEM((PLANES * rows, width), BF16),
             pltpu.VMEM((PLANES * rows, width), BF16),
             pltpu.VMEM((2, PLANES * rows, width), BF16),
-            pltpu.VMEM((2 * rows, width), BF16),
             dma((3,)),
             dma((6, PLANES)),
             dma((count,)),
@@ -505,7 +463,6 @@
             dma((PLANES, CHUNKS)),
             dma((PLANES, CHUNKS)),
             dma((2, PLANES, CHUNKS)),
-            dma((2, CHUNKS)),
         ],
         compiler_params=pltpu.CompilerParams(
             collective_id=0, has_side_effects=True, vmem_limit_bytes=60 * 1024 * 1024

time: 124 us -> 113 us (0.911)
  Pallas kernels: 120 us -> 108 us
    pallas_call x1, Pallas kernels: 120 us -> 108 us  [fused(): pl.pallas_call(fused_kernel, out_shape=(jax.ShapeDtypeStruct((rows, width...]
where the time goes in v4:
time: 113 us; the launch traced here: 112 us
  Pallas kernels  108 us (96%)
  local copies, waits for them, and re-layouts  3.29 us (3%)
  between operations  1.29 us (1%)
    pallas_call x1, Pallas kernels, fused(): pl.pallas_call(fused_kernel, out_shape=(jax.ShapeDtypeStruct((rows, width...  108 us
    unnamed x2, local copies, waits for them, and re-layouts  3.29 us

profile of v4, /device:TPU:0, one launch (start us, length us, event | category | flops | bytes accessed | tf_op | source)
XLA Modules:
  0.0 112.5 jit_solution(13623088699167225665)
XLA Ops:
  1.3 107.9 %shard_map.122 = (bf16[64,3584]{1,0:T(8,128)(2,1)}, bf16[1,64,512]{2,1,0:T(8,128)(2,1)}) custom-call(bf16[64,3584]{1,0:T(8,128)(2,1)} %tok_ref.1, s32[4,64]{1,0:T(4,128)} %bitcast.4, f32[4,64]{1,0:T(4,128)} %bitcast.5, bf16[3584,512]{1,0:T(8,128)(2,1)} %wg_hbm.1, bf16[3584,512]{1,0:T(8,128)(2,1)} %wu_hbm.1, bf16[512,3584]{1,0:T(8,128)(2,1)} %wd_hbm.1, ...), custom_call_target="tpu_custom_call" | custom-call | tf_op jit(solution)/shard_map/pallas_call | solution.py:437
  109.2 1.8 %copy.16 = bf16[64,3584]{1,0:T(8,128)(2,1)} copy(bf16[64,3584]{1,0:T(8,128)(2,1)} %get-tuple-element.4) | data formatting | bytes 917504
  111.0 1.5 %copy.17 = bf16[1,64,512]{2,1,0:T(8,128)(2,1)} copy(bf16[1,64,512]{2,1,0:T(8,128)(2,1)} %get-tuple-element.5) | data formatting | bytes 131072
